TPU v7x, 32 devices: a whole 2x2x4 slice. The times are simulated.
32 devices in a mesh: gx: 4 (over x, core), gy: 2 (over y), gz: 4 (over z).
Axes of the slice: x: 2, y: 2, z: 4, core: 2. Of those that a mesh axis runs over, the one named last changes fastest.
Arguments:
- magnet: float32 [3, 16, 128, 512], P(None, 'gz', 'gx', 'gy'), may hold values from -1 to 1, as said below
- grains: int32 [16, 128, 512], P('gz', 'gx', 'gy'), may hold values from 0 to 15
- stiffness_table: float32 [16], replicated, may hold values from 0.2 to 1
- saturation_table: float32 [16], replicated, may hold values from 0.6 to 1.4
- kernel_x: bfloat16 [8, 128], replicated, may hold values from -3 to 3
- kernel_y: bfloat16 [8, 512], replicated, may hold values from -3 to 3
- kernel_z: bfloat16 [8, 16], replicated, may hold values from -3 to 3
- mixing: float32 [8, 3, 3], replicated, may hold values from -1.25 to 1.25
Outputs:
- magnet_next: float32 [3, 16, 128, 512], P(None, 'gz', 'gx', 'gy')
- demag_field: float32 [8, 3, 64, 256], P('gz', None, 'gx', 'gy')
Inputs may be any that keep to these rules, and one draw needn't show every extreme that they name: `magnet`: every cell's three components form a unit vector.
All inputs are finite; a program needn't handle non-finite values.
Results may differ from a plain program's by a relative error of at most 0.00085.
The roundings to bfloat16 on the way count: a program that leaves them out, or rounds other values in their place, can miss the bound.
Values may be sent and summed in bfloat16 or wider, within the bound.
A program may use at most 128 MiB of HBM per device.

v0:
```python
import jax
import jax.numpy as jnp
from jax import lax
from jax.sharding import PartitionSpec as P

SUBSTEPS = 3


time_step = 0.02
damping = 0.3


def with_halo(x, sides, width):
    for axis, dim in sides:
        count, length = (lax.axis_size(axis), x.shape[dim])
        up = [(i, (i + 1) % count) for i in range(count - 1)]
        down = [(j, i) for i, j in up]
        last = lax.slice_in_dim(x, length - width, length, axis=dim)
        leading = lax.slice_in_dim(x, 0, width, axis=dim)
        before = lax.ppermute(last, axis, up)
        after = lax.ppermute(leading, axis, down)
        x = jnp.concatenate([before, x, after], axis=dim)
    return x


def toeplitz_rows(kernel, offset, extent):
    length = kernel.shape[1] // 2
    flipped = kernel[:, ::-1]
    row_ids = offset + jnp.arange(extent, dtype=jnp.int32)
    picked = jax.vmap(
        lambda row_index: lax.dynamic_slice_in_dim(flipped, length - 1 - row_index, length, 1)
    )(row_ids)
    return jnp.transpose(picked, (1, 0, 2))


def interior(values):
    return values[..., 1:-1, 1:-1, 1:-1]


def shifted(values, along, begin_at):
    slicer = [slice(1, -1), slice(1, -1), slice(1, -1)]
    slicer[along] = slice(begin_at, begin_at + values.shape[along - 3] - 2)
    leading = [slice(None)] * (values.ndim - 3)
    return values[tuple(leading + slicer)]


def cross_product(first_vec, second_vec):
    return jnp.stack(
        [
            first_vec[1] * second_vec[2] - first_vec[2] * second_vec[1],
            first_vec[2] * second_vec[0] - first_vec[0] * second_vec[2],
            first_vec[0] * second_vec[1] - first_vec[1] * second_vec[0],
        ]
    )


def exchange_update(magnet_rim, stiff_rim, saturation, demag_fine):
    centre = interior(magnet_rim)
    stiff_centre = interior(stiff_rim)
    coupled = jnp.zeros_like(centre)
    for along in range(3):
        for begin_at in (0, 2):
            stiff_near = shifted(stiff_rim, along, begin_at)
            denominator = stiff_centre + stiff_near
            weight = (
                2.0 * stiff_centre * stiff_near / jnp.where(denominator > 0.0, denominator, 1.0)
            )
            coupled = coupled + weight[None] * (shifted(magnet_rim, along, begin_at) - centre)
    inside = saturation > 0.0
    safe_sat = jnp.where(inside, saturation, 1.0)
    field_total = 2.0 * coupled / safe_sat[None] + demag_fine
    torque = cross_product(centre, field_total)
    raw_next = centre - time_step * (torque + damping * cross_product(centre, torque))
    length_sq = jnp.sqrt(jnp.sum(raw_next * raw_next, axis=0))
    safe_len = jnp.where(inside, length_sq, 1.0)
    return jnp.where(inside[None], raw_next / safe_len[None], 0.0)


def coarsen(magnet, saturation):
    weighted = saturation[None] * magnet
    comps, depth, width, height = weighted.shape
    shaped = weighted.reshape(comps, depth // 2, 2, width // 2, 2, height // 2, 2)
    return jnp.mean(shaped, axis=(2, 4, 6)).astype(jnp.bfloat16)


def prolong(demag):
    moved = jnp.transpose(demag, (1, 0, 2, 3))
    return jnp.repeat(jnp.repeat(jnp.repeat(moved, 2, axis=1), 2, axis=2), 2, axis=3)


def material_field(grains, lookup):
    labels = jnp.arange(lookup.shape[0], dtype=jnp.int32)
    matches = grains[None] == labels[:, None, None, None]
    return jnp.sum(jnp.where(matches, lookup[:, None, None, None], 0.0), axis=0)


def local(magnet, grains, stiffness_table, saturation_table, kernel_x, kernel_y, kernel_z, mixing):
    stiffness = material_field(grains, stiffness_table)
    saturation = material_field(grains, saturation_table)
    coarse = coarsen(magnet, saturation)
    rows_z = coarse.shape[1]
    rows_x = coarse.shape[2]
    rows_y = coarse.shape[3]
    block_x = toeplitz_rows(kernel_x, lax.axis_index("gx") * rows_x, rows_x)
    columns = block_x
    along_x = jnp.einsum(
        "rab,jzby->rjzay",
        columns,
        lax.all_gather(coarse, "gx", axis=2, tiled=True),
        preferred_element_type=jnp.float32,
    ).astype(jnp.bfloat16)
    block_y = toeplitz_rows(kernel_y, lax.axis_index("gy") * rows_y, rows_y)
    columns = block_y
    along_y = jnp.einsum(
        "rby,rjzxy->rjzxb",
        columns,
        lax.all_gather(along_x, "gy", axis=4, tiled=True),
        preferred_element_type=jnp.float32,
    ).astype(jnp.bfloat16)
    whole_z = toeplitz_rows(kernel_z, 0, kernel_z.shape[1] // 2).astype(jnp.float32)
    offset = lax.axis_index("gz") * rows_z
    own_rows = lax.dynamic_slice_in_dim(whole_z, offset, rows_z, 1)
    weights = jnp.einsum("rij,raz->airjz", mixing, own_rows, precision=lax.Precision.HIGHEST)
    columns = weights
    demag = jnp.einsum(
        "airjz,rjzxy->aixy",
        columns,
        lax.all_gather(along_y, "gz", axis=2, tiled=True).astype(jnp.float32),
        precision=lax.Precision.HIGHEST,
    )
    demag_fine = prolong(demag)
    stiff_rim = with_halo(
        stiffness[None].astype(jnp.bfloat16), (("gx", 2), ("gy", 3), ("gz", 1)), 1
    ).astype(jnp.float32)[0]
    state = magnet
    for substep in range(SUBSTEPS):
        magnet_rim = with_halo(state, (("gx", 2), ("gy", 3), ("gz", 1)), 1)
        state = exchange_update(magnet_rim, stiff_rim, saturation, demag_fine)
    return (state, demag)


def solution(mesh):
    in_specs = (P(None, "gz", "gx", "gy"), P("gz", "gx", "gy"), P(), P(), P(), P(), P(), P())
    out_specs = (P(None, "gz", "gx", "gy"), P("gz", None, "gx", "gy"))
    return jax.shard_map(local, mesh=mesh, in_specs=in_specs, out_specs=out_specs, check_vma=False)
```

profile of v0, /device:TPU:0, one launch (start us, length us, event | category | flops | bytes accessed | tf_op | source)
XLA Modules:
  0.0 376.2 jit_solution(11243058260585018113)
XLA Ops:
  2.9 3.0 collective-permute-start.6
  7.3 4.5 %collective-permute-start = (bf16[1,4,1,256]{3,2,1,0:T(2,128)(2,1)S(1)}, bf16[1,4,1,256]{3,2,1,0:T(2,128)(2,1)S(1)}, u32[]{:S(2)}, u32[]{:S(2)}) collective-permute-start(bf16[1,4,1,256]{3,2,1,0:T(2,128)(2,1)S(1)} %get-tuple-element.126), channel_id=1, source_target_pairs={{0,8},{8,16},{16,24},{1,9},{9,17},{17,25},{2,10},{10,18},{18,26},{... | collective-permute-start | bytes 6152 | tf_op jit(solution)/shard_map/ppermute | solution.py:20
  13.1 1.6 rev.11
  14.7 166.9 %while.5 = (s32[]{:T(128)}, bf16[8,512]{1,0:T(8,128)(2,1)S(1)}, s32[128,2]{0,1:T(2,128)S(1)}, bf16[128,8,256]{2,1,0:T(8,128)(2,1)S(1)}, s32[]{:T(128)}) while((s32[]{:T(128)}, bf16[8,512]{1,0:T(8,128)(2,1)S(1)}, s32[128,2]{0,1:T(2,128)S(1)}, bf16[128,8,256]{2,1,0:T(8,128)(2,1)S(1)}, s32[]{:T(128)}) %tuple.86), condition=%wide.while_cond.2, body=%wide.while_body.2.sunk | while | flops 2 | bytes 8297 | solution.py:31
  182.7 26.6 %reshape.132 = f32[3,2,2,16,2,128,2]{6,5,4,3,2,1,0:T(8,128)} reshape(f32[3,4,32,256]{3,2,1,0:T(8,128)S(1)} %broadcast_multiply_fusion) | data formatting | bytes 786432 | tf_op jit(solution)/shard_map/reshape | solution.py:82
  209.2 9.4 %reduce_sum.56 = f32[3,2,16,128]{3,2,1,0:T(8,128)S(1)} reduce(f32[3,2,2,16,2,128,2]{6,5,4,3,2,1,0:T(8,128)} %reshape.132, f32[]{:T(128)} %constant.20.clone.1), dimensions={2,4,6}, to_apply=%region_2.3 | reduce | flops 86016 | bytes 442372 | tf_op jit(solution)/shard_map/reduce_sum | solution.py:83
  218.7 6.1 %all_gather.9 = bf16[3,2,64,128]{3,2,1,0:T(8,128)(2,1)S(1)} all-gather(bf16[3,2,16,128]{3,2,1,0:T(8,128)(2,1)S(1)} %multiply_convert_fusion), channel_id=1, replica_groups=mesh['gx'=4,'gy'=2,'gz'=4] {'gx'}, dimensions={2}, use_global_device_ids=true | all-gather | bytes 122880 | tf_op jit(solution)/shard_map/all_gather | solution.py:109
  224.9 21.0 %while.4 = (s32[]{:T(128)}, bf16[8,128]{1,0:T(8,128)(2,1)S(1)}, s32[16,2]{0,1:T(2,128)S(1)}, bf16[16,8,64]{2,1,0:T(8,128)(2,1)S(1)}, s32[]{:T(128)}) while((s32[]{:T(128)}, bf16[8,128]{1,0:T(8,128)(2,1)S(1)}, s32[16,2]{0,1:T(2,128)S(1)}, bf16[16,8,64]{2,1,0:T(8,128)(2,1)S(1)}, s32[]{:T(128)}) %tuple.89), condition=%wide.while_cond.1, body=%wide.while_body.1.sunk | while | flops 2 | bytes 4201 | solution.py:31
  246.1 7.8 %all_gather.10 = bf16[8,3,2,16,256]{4,3,0,2,1:T(8,128)(2,1)S(1)} all-gather(bf16[8,3,2,16,128]{4,3,0,2,1:T(8,128)(2,1)S(1)} %fusion), channel_id=1, replica_groups=mesh['gx'=4,'gy'=2,'gz'=4] {'gy'}, dimensions={4}, use_global_device_ids=true | all-gather | bytes 589824 | tf_op jit(solution)/shard_map/all_gather | solution.py:117
  254.3 19.9 %all_gather.11 = bf16[8,3,8,16,128]{4,3,2,1,0:T(8,128)(2,1)S(1)} all-gather(bf16[8,3,2,16,128]{4,3,2,1,0:T(8,128)(2,1)S(1)} %convolution_convert_fusion.1), channel_id=1, replica_groups=mesh['gx'=4,'gy'=2,'gz'=4] {'gz'}, dimensions={2}, use_global_device_ids=true | all-gather | bytes 983040 | tf_op jit(solution)/shard_map/all_gather | solution.py:128
  274.4 10.5 %while.3 = (s32[]{:T(128)}, bf16[8,16]{1,0:T(8,128)(2,1)S(1)}, s32[8,2]{0,1:T(2,128)S(1)}, bf16[8,8,8]{2,1,0:T(8,128)(2,1)S(1)}, s32[]{:T(128)}) while((s32[]{:T(128)}, bf16[8,16]{1,0:T(8,128)(2,1)S(1)}, s32[8,2]{0,1:T(2,128)S(1)}, bf16[8,8,8]{2,1,0:T(8,128)(2,1)S(1)}, s32[]{:T(128)}) %tuple.92), condition=%wide.while_cond, body=%wide.while_body.sunk | while | flops 2 | bytes 4201 | solution.py:31
  284.9 1.4 fusion.1
  287.9 4.5 %collective-permute-start.2 = (bf16[1,4,34,1]{3,1,2,0:T(4,128)(2,1)S(1)}, bf16[1,4,34,1]{3,1,2,0:T(4,128)(2,1)S(1)}, u32[]{:S(2)}, u32[]{:S(2)}) collective-permute-start(bf16[1,4,34,1]{3,1,2,0:T(4,128)(2,1)S(1)} %get-tuple-element.123), channel_id=1, source_target_pairs={{0,4},{1,5},{2,6},{3,7},{8,12},{9,13},{10,14},{11,15},{16,20},{17,... | collective-permute-start | bytes 824 | tf_op jit(solution)/shard_map/ppermute | solution.py:20
  296.0 4.6 %collective-permute-start.8 = (f32[3,4,34,1]{3,1,2,0:T(4,128)S(1)}, f32[3,4,34,1]{3,1,2,0:T(4,128)S(1)}, u32[]{:S(2)}, u32[]{:S(2)}) collective-permute-start(f32[3,4,34,1]{3,1,2,0:T(4,128)S(1)} %get-tuple-element.107), channel_id=1, source_target_pairs={{0,4},{1,5},{2,6},{3,7},{8,12},{9,13},{10,14},{11,15},{16,20},{17,... | collective-permute-start | bytes 4904 | tf_op jit(solution)/shard_map/ppermute | solution.py:20
  302.0 4.5 %collective-permute-start.4 = (bf16[1,1,34,258]{3,2,1,0:T(8,128)(2,1)S(1)}, bf16[1,1,34,258]{3,2,1,0:T(8,128)(2,1)S(1)}, u32[]{:S(2)}, u32[]{:S(2)}) collective-permute-start(bf16[1,1,34,258]{3,2,1,0:T(8,128)(2,1)S(1)} %copy.551), channel_id=1, source_target_pairs={{0,1},{1,2},{2,3},{4,5},{5,6},{6,7},{8,9},{9,10},{10,11},{12,13},{... | collective-permute-start | bytes 52640 | tf_op jit(solution)/shard_map/ppermute | solution.py:20
  308.5 4.6 %collective-permute-start.10 = (f32[3,1,34,258]{3,2,1,0:T(8,128)S(1)}, f32[3,1,34,258]{3,2,1,0:T(8,128)S(1)}, u32[]{:S(2)}, u32[]{:S(2)}) collective-permute-start(f32[3,1,34,258]{3,2,1,0:T(8,128)S(1)} %get-tuple-element.95), channel_id=1, source_target_pairs={{0,1},{1,2},{2,3},{4,5},{5,6},{6,7},{8,9},{9,10},{10,11},{12,13},{... | collective-permute-start | bytes 315800 | tf_op jit(solution)/shard_map/ppermute | solution.py:20
  314.6 1.5 collective-permute-done.10
  320.0 3.7 collective-permute-done.13
  325.2 4.6 %collective-permute-start.14 = (f32[3,4,34,1]{3,1,2,0:T(4,128)S(1)}, f32[3,4,34,1]{3,1,2,0:T(4,128)S(1)}, u32[]{:S(2)}, u32[]{:S(2)}) collective-permute-start(f32[3,4,34,1]{3,1,2,0:T(4,128)S(1)} %get-tuple-element.103), channel_id=1, source_target_pairs={{0,4},{1,5},{2,6},{3,7},{8,12},{9,13},{10,14},{11,15},{16,20},{17,... | collective-permute-start | bytes 4904 | tf_op jit(solution)/shard_map/ppermute | solution.py:20
  329.8 2.5 collective-permute-done.15
  332.3 1.8 collective-permute-done.14
  336.0 5.2 %collective-permute-start.16 = (f32[3,1,34,258]{3,2,1,0:T(8,128)S(1)}, f32[3,1,34,258]{3,2,1,0:T(8,128)S(1)}, u32[]{:S(2)}, u32[]{:S(2)}) collective-permute-start(f32[3,1,34,258]{3,2,1,0:T(8,128)S(1)} %get-tuple-element.93), channel_id=1, source_target_pairs={{0,1},{1,2},{2,3},{4,5},{5,6},{6,7},{8,9},{9,10},{10,11},{12,13},{... | collective-permute-start | bytes 315800 | tf_op jit(solution)/shard_map/ppermute | solution.py:20
  341.8 2.2 collective-permute-done.17
  344.0 1.8 collective-permute-done.16
  346.8 2.3 collective-permute-start.18
  350.8 1.5 collective-permute-done.19
  353.7 4.6 %collective-permute-start.20 = (f32[3,4,34,1]{3,1,2,0:T(4,128)S(1)}, f32[3,4,34,1]{3,1,2,0:T(4,128)S(1)}, u32[]{:S(2)}, u32[]{:S(2)}) collective-permute-start(f32[3,4,34,1]{3,1,2,0:T(4,128)S(1)} %get-tuple-element.99), channel_id=1, source_target_pairs={{0,4},{1,5},{2,6},{3,7},{8,12},{9,13},{10,14},{11,15},{16,20},{17,... | collective-permute-start | bytes 4904 | tf_op jit(solution)/shard_map/ppermute | solution.py:20
  358.9 2.2 collective-permute-done.21
  361.1 1.8 collective-permute-done.20
  364.8 4.7 %collective-permute-start.22 = (f32[3,1,34,258]{3,2,1,0:T(8,128)S(1)}, f32[3,1,34,258]{3,2,1,0:T(8,128)S(1)}, u32[]{:S(2)}, u32[]{:S(2)}) collective-permute-start(f32[3,1,34,258]{3,2,1,0:T(8,128)S(1)} %get-tuple-element.91), channel_id=1, source_target_pairs={{0,1},{1,2},{2,3},{4,5},{5,6},{6,7},{8,9},{9,10},{10,11},{12,13},{... | collective-permute-start | bytes 315800 | tf_op jit(solution)/shard_map/ppermute | solution.py:20
  370.1 2.6 collective-permute-done.23
  372.7 1.7 collective-permute-done.22
  (587 shorter events, 231.5 us)
Async XLA Ops:
  1.6 292.9 %collective-permute-start.7 = (f32[3,4,1,256]{3,1,2,0:T(4,128)S(1)}, f32[3,4,1,256]{3,1,2,0:T(4,128)S(1)}, u32[]{:S(2)}, u32[]{:S(2)}) collective-permute-start(f32[3,4,1,256]{3,1,2,0:T(4,128)S(1)} %copy.548), channel_id=1, source_target_pairs={{8,0},{16,8},{24,16},{9,1},{17,9},{25,17},{10,2},{18,10},{26,18},{... | collective-permute-start | bytes 36872 | tf_op jit(solution)/shard_map/ppermute | solution.py:21
  2.9 291.2 %collective-permute-start.6 = (f32[3,4,1,256]{3,1,2,0:T(4,128)S(1)}, f32[3,4,1,256]{3,1,2,0:T(4,128)S(1)}, u32[]{:S(2)}, u32[]{:S(2)}) collective-permute-start(f32[3,4,1,256]{3,1,2,0:T(4,128)S(1)} %copy.549), channel_id=1, source_target_pairs={{0,8},{8,16},{16,24},{1,9},{9,17},{17,25},{2,10},{10,18},{18,26},{... | collective-permute-start | bytes 36872 | tf_op jit(solution)/shard_map/ppermute | solution.py:20
  7.3 279.0 %collective-permute-start = (bf16[1,4,1,256]{3,2,1,0:T(2,128)(2,1)S(1)}, bf16[1,4,1,256]{3,2,1,0:T(2,128)(2,1)S(1)}, u32[]{:S(2)}, u32[]{:S(2)}) collective-permute-start(bf16[1,4,1,256]{3,2,1,0:T(2,128)(2,1)S(1)} %get-tuple-element.126), channel_id=1, source_target_pairs={{0,8},{8,16},{16,24},{1,9},{9,17},{17,25},{2,10},{10,18},{18,26},{... | collective-permute-start | bytes 6152 | tf_op jit(solution)/shard_map/ppermute | solution.py:20
  11.8 274.7 %collective-permute-start.1 = (bf16[1,4,1,256]{3,2,1,0:T(2,128)(2,1)S(1)}, bf16[1,4,1,256]{3,2,1,0:T(2,128)(2,1)S(1)}, u32[]{:S(2)}, u32[]{:S(2)}) collective-permute-start(bf16[1,4,1,256]{3,2,1,0:T(2,128)(2,1)S(1)} %get-tuple-element.125), channel_id=1, source_target_pairs={{8,0},{16,8},{24,16},{9,1},{17,9},{25,17},{10,2},{18,10},{26,18},{... | collective-permute-start | bytes 6152 | tf_op jit(solution)/shard_map/ppermute | solution.py:21
  209.2 15.6 %copy-start.2 = (bf16[8,128]{1,0:T(8,128)(2,1)S(1)}, bf16[8,128]{1,0:T(8,128)(2,1)}, u32[]{:S(2)}) copy-start(bf16[8,128]{1,0:T(8,128)(2,1)} %param.12) | copy-start | bytes 6148
  218.6 55.6 %copy-start.1 = (f32[8,3,3]{0,2,1:T(4,128)S(1)}, f32[8,3,3]{0,2,1:T(4,128)}, u32[]{:S(2)}) copy-start(f32[8,3,3]{0,2,1:T(4,128)} %param.15) | copy-start | bytes 868
  218.7 55.7 %copy-start.3 = (bf16[8,16]{1,0:T(8,128)(2,1)S(1)}, bf16[8,16]{1,0:T(8,128)(2,1)}, u32[]{:S(2)}) copy-start(bf16[8,16]{1,0:T(8,128)(2,1)} %param.14) | copy-start | bytes 772
  286.6 7.2 %collective-permute-start.3 = (bf16[1,4,34,1]{3,1,2,0:T(4,128)(2,1)S(1)}, bf16[1,4,34,1]{3,1,2,0:T(4,128)(2,1)S(1)}, u32[]{:S(2)}, u32[]{:S(2)}) collective-permute-start(bf16[1,4,34,1]{3,1,2,0:T(4,128)(2,1)S(1)} %get-tuple-element.124), channel_id=1, source_target_pairs={{4,0},{5,1},{6,2},{7,3},{12,8},{13,9},{14,10},{15,11},{20,16},{21,... | collective-permute-start | bytes 824 | tf_op jit(solution)/shard_map/ppermute | solution.py:21
  287.9 6.2 %collective-permute-start.2 = (bf16[1,4,34,1]{3,1,2,0:T(4,128)(2,1)S(1)}, bf16[1,4,34,1]{3,1,2,0:T(4,128)(2,1)S(1)}, u32[]{:S(2)}, u32[]{:S(2)}) collective-permute-start(bf16[1,4,34,1]{3,1,2,0:T(4,128)(2,1)S(1)} %get-tuple-element.123), channel_id=1, source_target_pairs={{0,4},{1,5},{2,6},{3,7},{8,12},{9,13},{10,14},{11,15},{16,20},{17,... | collective-permute-start | bytes 824 | tf_op jit(solution)/shard_map/ppermute | solution.py:20
  292.8 1.4 copy-start
  294.7 11.9 %collective-permute-start.9 = (f32[3,4,34,1]{3,1,2,0:T(4,128)S(1)}, f32[3,4,34,1]{3,1,2,0:T(4,128)S(1)}, u32[]{:S(2)}, u32[]{:S(2)}) collective-permute-start(f32[3,4,34,1]{3,1,2,0:T(4,128)S(1)} %get-tuple-element.108), channel_id=1, source_target_pairs={{4,0},{5,1},{6,2},{7,3},{12,8},{13,9},{14,10},{15,11},{20,16},{21,... | collective-permute-start | bytes 4904 | tf_op jit(solution)/shard_map/ppermute | solution.py:21
  296.0 10.6 %collective-permute-start.8 = (f32[3,4,34,1]{3,1,2,0:T(4,128)S(1)}, f32[3,4,34,1]{3,1,2,0:T(4,128)S(1)}, u32[]{:S(2)}, u32[]{:S(2)}) collective-permute-start(f32[3,4,34,1]{3,1,2,0:T(4,128)S(1)} %get-tuple-element.107), channel_id=1, source_target_pairs={{0,4},{1,5},{2,6},{3,7},{8,12},{9,13},{10,14},{11,15},{16,20},{17,... | collective-permute-start | bytes 4904 | tf_op jit(solution)/shard_map/ppermute | solution.py:20
  300.7 13.0 %collective-permute-start.5 = (bf16[1,1,34,258]{3,2,1,0:T(8,128)(2,1)S(1)}, bf16[1,1,34,258]{3,2,1,0:T(8,128)(2,1)S(1)}, u32[]{:S(2)}, u32[]{:S(2)}) collective-permute-start(bf16[1,1,34,258]{3,2,1,0:T(8,128)(2,1)S(1)} %copy.550), channel_id=1, source_target_pairs={{1,0},{2,1},{3,2},{5,4},{6,5},{7,6},{9,8},{10,9},{11,10},{13,12},{... | collective-permute-start | bytes 52640 | tf_op jit(solution)/shard_map/ppermute | solution.py:21
  302.0 11.7 %collective-permute-start.4 = (bf16[1,1,34,258]{3,2,1,0:T(8,128)(2,1)S(1)}, bf16[1,1,34,258]{3,2,1,0:T(8,128)(2,1)S(1)}, u32[]{:S(2)}, u32[]{:S(2)}) collective-permute-start(bf16[1,1,34,258]{3,2,1,0:T(8,128)(2,1)S(1)} %copy.551), channel_id=1, source_target_pairs={{0,1},{1,2},{2,3},{4,5},{5,6},{6,7},{8,9},{9,10},{10,11},{12,13},{... | collective-permute-start | bytes 52640 | tf_op jit(solution)/shard_map/ppermute | solution.py:20
  307.2 7.4 %collective-permute-start.11 = (f32[3,1,34,258]{3,2,1,0:T(8,128)S(1)}, f32[3,1,34,258]{3,2,1,0:T(8,128)S(1)}, u32[]{:S(2)}, u32[]{:S(2)}) collective-permute-start(f32[3,1,34,258]{3,2,1,0:T(8,128)S(1)} %get-tuple-element.96), channel_id=1, source_target_pairs={{1,0},{2,1},{3,2},{5,4},{6,5},{7,6},{9,8},{10,9},{11,10},{13,12},{... | collective-permute-start | bytes 315800 | tf_op jit(solution)/shard_map/ppermute | solution.py:21
  308.5 7.6 %collective-permute-start.10 = (f32[3,1,34,258]{3,2,1,0:T(8,128)S(1)}, f32[3,1,34,258]{3,2,1,0:T(8,128)S(1)}, u32[]{:S(2)}, u32[]{:S(2)}) collective-permute-start(f32[3,1,34,258]{3,2,1,0:T(8,128)S(1)} %get-tuple-element.95), channel_id=1, source_target_pairs={{0,1},{1,2},{2,3},{4,5},{5,6},{6,7},{8,9},{9,10},{10,11},{12,13},{... | collective-permute-start | bytes 315800 | tf_op jit(solution)/shard_map/ppermute | solution.py:20
  317.1 2.6 collective-permute-start.12
  318.4 5.3 %collective-permute-start.13 = (f32[3,4,1,256]{3,1,2,0:T(4,128)S(1)}, f32[3,4,1,256]{3,1,2,0:T(4,128)S(1)}, u32[]{:S(2)}, u32[]{:S(2)}) collective-permute-start(f32[3,4,1,256]{3,1,2,0:T(4,128)S(1)} %copy.455), channel_id=1, source_target_pairs={{8,0},{16,8},{24,16},{9,1},{17,9},{25,17},{10,2},{18,10},{26,18},{... | collective-permute-start | bytes 36872 | tf_op jit(solution)/shard_map/ppermute | solution.py:21
  323.9 8.4 %collective-permute-start.15 = (f32[3,4,34,1]{3,1,2,0:T(4,128)S(1)}, f32[3,4,34,1]{3,1,2,0:T(4,128)S(1)}, u32[]{:S(2)}, u32[]{:S(2)}) collective-permute-start(f32[3,4,34,1]{3,1,2,0:T(4,128)S(1)} %get-tuple-element.104), channel_id=1, source_target_pairs={{4,0},{5,1},{6,2},{7,3},{12,8},{13,9},{14,10},{15,11},{20,16},{21,... | collective-permute-start | bytes 4904 | tf_op jit(solution)/shard_map/ppermute | solution.py:21
  325.2 8.9 %collective-permute-start.14 = (f32[3,4,34,1]{3,1,2,0:T(4,128)S(1)}, f32[3,4,34,1]{3,1,2,0:T(4,128)S(1)}, u32[]{:S(2)}, u32[]{:S(2)}) collective-permute-start(f32[3,4,34,1]{3,1,2,0:T(4,128)S(1)} %get-tuple-element.103), channel_id=1, source_target_pairs={{0,4},{1,5},{2,6},{3,7},{8,12},{9,13},{10,14},{11,15},{16,20},{17,... | collective-permute-start | bytes 4904 | tf_op jit(solution)/shard_map/ppermute | solution.py:20
  334.7 9.3 %collective-permute-start.17 = (f32[3,1,34,258]{3,2,1,0:T(8,128)S(1)}, f32[3,1,34,258]{3,2,1,0:T(8,128)S(1)}, u32[]{:S(2)}, u32[]{:S(2)}) collective-permute-start(f32[3,1,34,258]{3,2,1,0:T(8,128)S(1)} %get-tuple-element.94), channel_id=1, source_target_pairs={{1,0},{2,1},{3,2},{5,4},{6,5},{7,6},{9,8},{10,9},{11,10},{13,12},{... | collective-permute-start | bytes 315800 | tf_op jit(solution)/shard_map/ppermute | solution.py:21
  336.0 9.8 %collective-permute-start.16 = (f32[3,1,34,258]{3,2,1,0:T(8,128)S(1)}, f32[3,1,34,258]{3,2,1,0:T(8,128)S(1)}, u32[]{:S(2)}, u32[]{:S(2)}) collective-permute-start(f32[3,1,34,258]{3,2,1,0:T(8,128)S(1)} %get-tuple-element.93), channel_id=1, source_target_pairs={{0,1},{1,2},{2,3},{4,5},{5,6},{6,7},{8,9},{9,10},{10,11},{12,13},{... | collective-permute-start | bytes 315800 | tf_op jit(solution)/shard_map/ppermute | solution.py:20
  346.8 3.6 collective-permute-start.18
  349.1 3.1 collective-permute-start.19
  352.4 8.7 %collective-permute-start.21 = (f32[3,4,34,1]{3,1,2,0:T(4,128)S(1)}, f32[3,4,34,1]{3,1,2,0:T(4,128)S(1)}, u32[]{:S(2)}, u32[]{:S(2)}) collective-permute-start(f32[3,4,34,1]{3,1,2,0:T(4,128)S(1)} %get-tuple-element.100), channel_id=1, source_target_pairs={{4,0},{5,1},{6,2},{7,3},{12,8},{13,9},{14,10},{15,11},{20,16},{21,... | collective-permute-start | bytes 4904 | tf_op jit(solution)/shard_map/ppermute | solution.py:21
  353.7 9.2 %collective-permute-start.20 = (f32[3,4,34,1]{3,1,2,0:T(4,128)S(1)}, f32[3,4,34,1]{3,1,2,0:T(4,128)S(1)}, u32[]{:S(2)}, u32[]{:S(2)}) collective-permute-start(f32[3,4,34,1]{3,1,2,0:T(4,128)S(1)} %get-tuple-element.99), channel_id=1, source_target_pairs={{0,4},{1,5},{2,6},{3,7},{8,12},{9,13},{10,14},{11,15},{16,20},{17,... | collective-permute-start | bytes 4904 | tf_op jit(solution)/shard_map/ppermute | solution.py:20
  363.5 9.2 %collective-permute-start.23 = (f32[3,1,34,258]{3,2,1,0:T(8,128)S(1)}, f32[3,1,34,258]{3,2,1,0:T(8,128)S(1)}, u32[]{:S(2)}, u32[]{:S(2)}) collective-permute-start(f32[3,1,34,258]{3,2,1,0:T(8,128)S(1)} %get-tuple-element.92), channel_id=1, source_target_pairs={{1,0},{2,1},{3,2},{5,4},{6,5},{7,6},{9,8},{10,9},{11,10},{13,12},{... | collective-permute-start | bytes 315800 | tf_op jit(solution)/shard_map/ppermute | solution.py:21
  364.8 9.6 %collective-permute-start.22 = (f32[3,1,34,258]{3,2,1,0:T(8,128)S(1)}, f32[3,1,34,258]{3,2,1,0:T(8,128)S(1)}, u32[]{:S(2)}, u32[]{:S(2)}) collective-permute-start(f32[3,1,34,258]{3,2,1,0:T(8,128)S(1)} %get-tuple-element.91), channel_id=1, source_target_pairs={{0,1},{1,2},{2,3},{4,5},{5,6},{6,7},{8,9},{9,10},{10,11},{12,13},{... | collective-permute-start | bytes 315800 | tf_op jit(solution)/shard_map/ppermute | solution.py:20
where the time goes:
time: 380 us; the launch traced here: 376 us
  local copies, waits for them, and re-layouts  232 us (61%)
  starting transfers between devices  63.8 us (17%)
  blocking collectives  33.9 us (9%)
  waiting for transfers between devices  24 us (6%)
  other arithmetic  19.2 us (5%)
    gather x456, local copies, waits for them, and re-layouts  198 us
    ppermute x12, starting transfers between devices, with_halo(): before = lax.ppermute(last, axis, up)  48.3 us
    reshape x1, local copies, waits for them, and re-layouts, coarsen(): weighted.reshape(comps, depth // 2, 2, width // 2, 2, height // 2, 2)  26.6 us
    all_gather x1, blocking collectives, local(): lax.all_gather(along_y, 'gz', axis=2, tiled=True).astype(jnp.float32)  19.9 us
    ppermute x12, starting transfers between devices, with_halo(): after = lax.ppermute(leading, axis, down)  15.5 us
    ppermute x12, waiting for transfers between devices, with_halo(): after = lax.ppermute(leading, axis, down)  15.3 us
    reduce_sum x1, other arithmetic, coarsen(): return jnp.mean(shaped, axis=(2, 4, 6)).astype(jnp.bfloat16)  9.41 us
    ppermute x12, waiting for transfers between devices, with_halo(): before = lax.ppermute(last, axis, up)  8.7 us
  transfers between devices with their start and end apart: 24, of which 13 were waited for; matrix products, arithmetic and copies ran while one was open for 65% of the time, Pallas kernels for 0%

commit v1 on v0

v1 whole, which is shorter than its diff:
```python
import functools

import jax
import jax.numpy as jnp
from jax import lax
from jax.experimental import pallas as pl
from jax.experimental.pallas import tpu as pltpu
from jax.sharding import PartitionSpec as P

SUBSTEPS = 3
TIME_STEP = 0.02
DAMPING = 0.3
LANES = 128
HIGHEST = lax.Precision.HIGHEST
MESH = pl.DeviceIdType.MESH
F32 = jnp.float32
BF16 = jnp.bfloat16


def kernel(
    dims,
    magnet, grains, stiff_tab, sat_tab, kx, ky, kz, mix,
    out_m, out_d,
    state, stiff, inv_sat, weights, pooled_in, pooled, gathered, kx32, ky32, kz32, flat_x,
    mat_x, mat_y, trans_x, mixed, z_send, z_recv, fine,
    xs, xr, ys, yr, zs, zr,
    g_send, g_recv, s_send, s_recv, h_send, h_recv,
):
    cx, cy, cz = dims
    comps, nz, nx, ny = magnet.shape
    rank = kx.shape[0]
    mats = stiff_tab.shape[0]
    rz, rx, ry = nz // 2, nx // 2, ny // 2
    gx_all, gy_all, gz_all = rx * cx, ry * cy, rz * cz
    jz = comps * rz
    ix, iy, iz = lax.axis_index("gx"), lax.axis_index("gy"), lax.axis_index("gz")
    plane = cx * cy
    me = ix * cy + iy

    def spot(number):
        return lax.div(number, cy), lax.rem(number, cy)

    barrier = pltpu.get_barrier_semaphore()
    for d in range(1, plane):
        tx, ty = spot(lax.rem(me + d, plane))
        pl.semaphore_signal(
            barrier, inc=1, device_id={"gx": tx, "gy": ty, "gz": iz}, device_id_type=MESH
        )
    for d in range(1, cz):
        pl.semaphore_signal(
            barrier, inc=1,
            device_id={"gx": ix, "gy": iy, "gz": lax.rem(iz + d, cz)}, device_id_type=MESH,
        )

    row = lax.broadcasted_iota(jnp.int32, (nx, ny), 0)
    lane = lax.broadcasted_iota(jnp.int32, (nx, ny), 1)
    pack_lane = lax.broadcasted_iota(jnp.int32, (nx, LANES), 1)

    for zc in range(rz):
        sums = [None] * comps
        for half in range(2):
            z = 2 * zc + half
            g = grains[z]
            a = jnp.full((nx, ny), stiff_tab[0], F32)
            s = jnp.full((nx, ny), sat_tab[0], F32)
            for k in range(1, mats):
                hit = g == k
                a = jnp.where(hit, stiff_tab[k], a)
                s = jnp.where(hit, sat_tab[k], s)
            stiff[z] = a
            inv_sat[z] = 2.0 / s
            for j in range(comps):
                m = magnet[j, z]
                state[0, j, z + 1] = m
                sums[j] = s * m if half == 0 else sums[j] + s * m
        for j in range(comps):
            pooled_in[(j * rz + zc) * nx:(j * rz + zc + 1) * nx, :] = sums[j]
    fold = (
        lax.broadcasted_iota(jnp.int32, (ny, ry), 0) // 2
        == lax.broadcasted_iota(jnp.int32, (ny, ry), 1)
    ).astype(F32)
    pooled[...] = jnp.dot(
        pooled_in[...], fold, precision=HIGHEST, preferred_element_type=F32
    )
    coarse = 0.125 * (
        pooled[pl.ds(0, jz * rx, 2), :] + pooled[pl.ds(1, jz * rx, 2), :]
    )

    def block_of(px, py):
        return gathered.at[
            :, pl.ds(pl.multiple_of(px * rx, rx), rx), pl.ds(pl.multiple_of(py * ry, ry), ry)
        ]

    block_of(ix, iy)[...] = coarse.astype(BF16).reshape(jz, rx, ry)

    def pack(step, k, value, edges):
        xs[step, 0, k:k + 1, :] = value[0:1, :]
        xs[step, 1, k:k + 1, :] = value[nx - 1:nx, :]
        hit = pack_lane == k
        return (
            jnp.where(hit, value[:, 0:1], edges[0]),
            jnp.where(hit, value[:, ny - 1:ny], edges[1]),
        )

    edges = (jnp.zeros((nx, LANES), F32),) * 2
    for j in range(comps + 1):
        for z in range(nz):
            value = magnet[j, z] if j < comps else stiff[z]
            edges = pack(0, j * nz + z, value, edges)
            if z == 0:
                zs[0, 0, j] = value.astype(BF16)
            if z == nz - 1:
                zs[0, 1, j] = value.astype(BF16)
    ys[0, 0], ys[0, 1] = edges

    pl.semaphore_wait(barrier, plane - 1 + cz - 1)

    def gather_copy(d, source):
        px, py = spot(source)
        tx, ty = spot(lax.rem(me + d, plane))
        return pltpu.make_async_remote_copy(
            src_ref=block_of(px, py), dst_ref=block_of(px, py),
            send_sem=g_send.at[d - 1], recv_sem=g_recv.at[d - 1],
            device_id={"gx": tx, "gy": ty, "gz": iz}, device_id_type=MESH,
        )

    for d in range(1, plane):
        gather_copy(d, me).start()

    places = (ix, iy, iz)
    counts = (cx, cy, cz)
    names = ("gx", "gy", "gz")

    def halo_copy(step, axis, way):
        sends, recvs = ((xs, xr), (ys, yr), (zs, zr))[axis]
        src, dst = sends.at[step, way], recvs.at[step, 1 - way]
        if axis == 2 and step > 0:
            src, dst = src.at[0:comps], dst.at[0:comps]
        target = dict(zip(names, places))
        target[names[axis]] = places[axis] + (2 * way - 1)
        return pltpu.make_async_remote_copy(
            src_ref=src, dst_ref=dst,
            send_sem=h_send.at[step, axis, way], recv_sem=h_recv.at[step, axis, way],
            device_id=target, device_id_type=MESH,
        )

    def can_send(axis, way):
        return places[axis] > 0 if way == 0 else places[axis] < counts[axis] - 1

    def send_halos(step):
        for axis in (2, 1, 0):
            for way in range(2):
                @pl.when(can_send(axis, way))
                def _():
                    halo_copy(step, axis, way).start()

    def receive_halos(step):
        for axis in range(3):
            for way in range(2):
                @pl.when(can_send(axis, 1 - way))
                def _():
                    halo_copy(step, axis, way).wait_recv()

    send_halos(0)

    for axis in range(3):
        recvs = (xr, yr, zr)[axis]
        for way in range(2):
            @pl.when(jnp.logical_not(can_send(axis, way)))
            def _():
                for step in range(SUBSTEPS):
                    recvs[step, way] = jnp.zeros(recvs.shape[2:], recvs.dtype)

    kx32[...] = kx[...].astype(F32)
    ky32[...] = ky[...].astype(F32)
    kz32[...] = jnp.zeros_like(kz32)
    kz32[:, 0:kz.shape[1]] = kz[...].astype(F32)

    def skewed(line, width):
        rows = jnp.broadcast_to(line, (8, width))
        place = lax.broadcasted_iota(jnp.int32, (8, width), 0)
        for step in (1, 2, 4):
            rows = jnp.where(place & step != 0, pltpu.roll(rows, step, 1), rows)
        return rows

    wide = 2 * gx_all
    lane_x = lax.broadcasted_iota(jnp.int32, (8, wide), 1)
    kx_here = pltpu.roll(kx32[...], lax.rem(2 * wide - gx_all - ix * rx, wide), 1)
    bases = [skewed(kx_here[r:r + 1, :], wide) for r in range(rank)]
    for t in range(gx_all // 8):
        block = jnp.zeros((8, wide), F32)
        for r in range(rank):
            turned = pltpu.roll(bases[r], (8 * t + r * rx) % wide, 1)
            block = jnp.where(lane_x // rx == r, turned, block)
        flat_x[8 * t:8 * t + 8, :] = block[:, 0:rank * rx]
    mat_x[...] = jnp.transpose(flat_x[...]).astype(BF16)
    for c in range(cy):
        start = pl.multiple_of(ry * (iy - c) + gy_all - ry, ry)
        window = ky32[:, pl.ds(start, 2 * ry)]
        for r in range(rank):
            base = skewed(window[r:r + 1, :], 2 * ry)
            for t in range(0, ry // 8, 2):
                pair = jnp.concatenate(
                    [pltpu.roll(base, 8 * (t + e) + ry, 1)[:, 0:ry] for e in range(2)], axis=0
                )
                mat_y[r, c * ry + 8 * t:c * ry + 8 * t + 16, :] = pair.astype(BF16)

    for d in range(1, plane):
        gather_copy(d, lax.rem(me + plane - d, plane)).wait_recv()

    for t in range(jz):
        along = jnp.dot(mat_x[...], gathered[t], preferred_element_type=F32).astype(BF16)
        trans_x[:, t * rx:(t + 1) * rx, :] = along.reshape(rank, rx, gy_all)
    for r in range(rank):
        along = jnp.dot(trans_x[r], mat_y[r], preferred_element_type=F32)
        along = along.astype(BF16).astype(F32).reshape(comps, rz, rx, ry)
        for i in range(comps):
            total = mix[r, i, 0] * along[0]
            for j in range(1, comps):
                total = total + mix[r, i, j] * along[j]
            mixed[r, i] = total
    turned_z = pltpu.roll(kz32[...], lax.rem(LANES + rz - 1 + rz * iz - gz_all, LANES), 1)

    def sum_copy(peer, slot):
        return pltpu.make_async_remote_copy(
            src_ref=z_send.at[peer], dst_ref=z_recv.at[slot],
            send_sem=s_send.at[peer], recv_sem=s_recv.at[slot],
            device_id={"gx": ix, "gy": iy, "gz": jnp.int32(peer)}, device_id_type=MESH,
        )

    for p in range(cz):
        totals = [[jnp.zeros((rx, ry), F32) for _ in range(comps)] for _ in range(rz)]
        for r in range(rank):
            for al in range(rz):
                for zl in range(rz):
                    at = p * rz + al - zl + rz - 1
                    factor = turned_z[r:r + 1, at:at + 1]
                    for i in range(comps):
                        totals[al][i] = totals[al][i] + factor * mixed[r, i, zl]
        for al in range(rz):
            for i in range(comps):
                z_send[p, al, i] = totals[al][i]

        @pl.when(iz != p)
        def _():
            sum_copy(p, iz).start()

        @pl.when(iz == p)
        def _():
            z_recv[p] = z_send[p]

    receive_halos(0)

    def around(value, step, k):
        return (
            jnp.where(row == 0, xr[step, 0, k:k + 1, :], pltpu.roll(value, 1, 0)),
            jnp.where(row == nx - 1, xr[step, 1, k:k + 1, :], pltpu.roll(value, nx - 1, 0)),
            jnp.where(lane == 0, yr[step, 0][:, k:k + 1], pltpu.roll(value, 1, 1)),
            jnp.where(lane == ny - 1, yr[step, 1][:, k:k + 1], pltpu.roll(value, ny - 1, 1)),
        )

    for z in range(nz):
        here = stiff[z]
        below = zr[0, 0, comps].astype(F32) if z == 0 else stiff[z - 1]
        above = zr[0, 1, comps].astype(F32) if z == nz - 1 else stiff[z + 1]
        scale = 2.0 * inv_sat[z] * here
        for n, near in enumerate(around(here, 0, comps * nz + z) + (below, above)):
            weights[n, z] = scale * near / (here + near)

    for p in range(cz):
        @pl.when(iz != p)
        def _():
            sum_copy(p, p).wait_recv()

    total = z_recv[0]
    for p in range(1, cz):
        total = total + z_recv[p]
    out_d[...] = total
    unfold = (
        lax.broadcasted_iota(jnp.int32, (ry, ny), 1) // 2
        == lax.broadcasted_iota(jnp.int32, (ry, ny), 0)
    ).astype(F32)
    spread = jnp.dot(
        total.reshape(rz * comps * rx, ry), unfold, precision=HIGHEST,
        preferred_element_type=F32,
    )
    for part in range(2):
        piece = spread[:, part * ry:(part + 1) * ry]
        for odd in range(2):
            fine.at[part][pl.ds(odd, rz * comps * rx, 2), :] = piece

    for step in range(SUBSTEPS):
        now, later = step % 2, (step + 1) % 2
        last = step == SUBSTEPS - 1
        if step > 0:
            receive_halos(step)
        for j in range(comps):
            state[now, j, 0] = zr[step, 0, j].astype(F32)
            state[now, j, nz + 1] = zr[step, 1, j].astype(F32)
        edges = (jnp.zeros((nx, LANES), F32),) * 2
        for z in range(nz):
            m, h = [], []
            for j in range(comps):
                value = state[now, j, z + 1]
                at = ((z // 2) * comps + j) * nx
                field = jnp.concatenate([fine[0, at:at + nx, :], fine[1, at:at + nx, :]], axis=1)
                near = around(value, step, j * nz + z) + (
                    state[now, j, z], state[now, j, z + 2]
                )
                for n in range(6):
                    field = field + weights[n, z] * near[n]
                m.append(value)
                h.append(field)
            t = [
                m[1] * h[2] - m[2] * h[1],
                m[2] * h[0] - m[0] * h[2],
                m[0] * h[1] - m[1] * h[0],
            ]
            u = [
                m[1] * t[2] - m[2] * t[1],
                m[2] * t[0] - m[0] * t[2],
                m[0] * t[1] - m[1] * t[0],
            ]
            raw = [m[j] - TIME_STEP * (t[j] + DAMPING * u[j]) for j in range(comps)]
            shrink = lax.rsqrt(raw[0] * raw[0] + raw[1] * raw[1] + raw[2] * raw[2])
            for j in range(comps):
                value = raw[j] * shrink
                if last:
                    out_m[j, z] = value
                    continue
                state[later, j, z + 1] = value
                edges = pack(step + 1, j * nz + z, value, edges)
                if z == 0:
                    zs[step + 1, 0, j] = value.astype(BF16)
                if z == nz - 1:
                    zs[step + 1, 1, j] = value.astype(BF16)
        if not last:
            ys[step + 1, 0], ys[step + 1, 1] = edges
            send_halos(step + 1)

    for d in range(1, plane):
        gather_copy(d, me).wait_send()
    for p in range(cz):
        @pl.when(iz != p)
        def _():
            sum_copy(p, iz).wait_send()
    for step in range(SUBSTEPS):
        for axis in range(3):
            for way in range(2):
                @pl.when(can_send(axis, way))
                def _():
                    halo_copy(step, axis, way).wait_send()


def local(dims, magnet, grains, stiff_tab, sat_tab, kx, ky, kz, mix):
    cx, cy, cz = dims
    comps, nz, nx, ny = magnet.shape
    rank = kx.shape[0]
    rz, rx, ry = nz // 2, nx // 2, ny // 2
    jz = comps * rz
    gx_all, gy_all = rx * cx, ry * cy
    packed = (comps + 1) * nz
    vmem = pl.BlockSpec(memory_space=pltpu.VMEM)
    smem = pl.BlockSpec(memory_space=pltpu.SMEM)
    dma = pltpu.SemaphoreType.DMA
    return pl.pallas_call(
        functools.partial(kernel, dims),
        out_shape=(
            jax.ShapeDtypeStruct(magnet.shape, F32),
            jax.ShapeDtypeStruct((rz, comps, rx, ry), F32),
        ),
        in_specs=[vmem, vmem, smem, smem, vmem, vmem, vmem, smem],
        out_specs=(vmem, vmem),
        scratch_shapes=[
            pltpu.VMEM((2, comps, nz + 2, nx, ny), F32),
            pltpu.VMEM((nz, nx, ny), F32),
            pltpu.VMEM((nz, nx, ny), F32),
            pltpu.VMEM((6, nz, nx, ny), F32),
            pltpu.VMEM((jz * nx, ny), F32),
            pltpu.VMEM((jz * nx, ry), F32),
            pltpu.VMEM((jz, gx_all, gy_all), BF16),
            pltpu.VMEM(kx.shape, F32),
            pltpu.VMEM(ky.shape, F32),
            pltpu.VMEM((rank, LANES), F32),
            pltpu.VMEM((gx_all, rank * rx), F32),
            pltpu.VMEM((rank * rx, gx_all), BF16),
            pltpu.VMEM((rank, gy_all, ry), BF16),
            pltpu.VMEM((rank, jz * rx, gy_all), BF16),
            pltpu.VMEM((rank, comps, rz, rx, ry), F32),
            pltpu.VMEM((cz, rz, comps, rx, ry), F32),
            pltpu.VMEM((cz, rz, comps, rx, ry), F32),
            pltpu.VMEM((2, jz * nx, ry), F32),
            pltpu.VMEM((SUBSTEPS, 2, packed, ny), F32),
            pltpu.VMEM((SUBSTEPS, 2, packed, ny), F32),
            pltpu.VMEM((SUBSTEPS, 2, nx, LANES), F32),
            pltpu.VMEM((SUBSTEPS, 2, nx, LANES), F32),
            pltpu.VMEM((SUBSTEPS, 2, comps + 1, nx, ny), BF16),
            pltpu.VMEM((SUBSTEPS, 2, comps + 1, nx, ny), BF16),
            dma((cx * cy - 1,)),
            dma((cx * cy - 1,)),
            dma((cz,)),
            dma((cz,)),
            dma((SUBSTEPS, 3, 2)),
            dma((SUBSTEPS, 3, 2)),
        ],
        compiler_params=pltpu.CompilerParams(
            collective_id=0, has_side_effects=True, vmem_limit_bytes=40 * 1024 * 1024
        ),
    )(magnet, grains, stiff_tab, sat_tab, kx, ky, kz, mix)


def solution(mesh):
    dims = tuple(mesh.shape[name] for name in ("gx", "gy", "gz"))
    in_specs = (P(None, "gz", "gx", "gy"), P("gz", "gx", "gy"), P(), P(), P(), P(), P(), P())
    out_specs = (P(None, "gz", "gx", "gy"), P("gz", None, "gx", "gy"))
    return jax.shard_map(
        functools.partial(local, dims), mesh=mesh, in_specs=in_specs, out_specs=out_specs,
        check_vma=False,
    )
```

time: 380 us -> 30.5 us (0.08)
  local copies, waits for them, and re-layouts: 232 us -> 4.1 us
  starting transfers between devices: 63.8 us -> 0 us
  blocking collectives: 33.9 us -> 0 us
  Pallas kernels: 0 us -> 25.4 us
  waiting for transfers between devices: 24 us -> 0 us
  other arithmetic: 19.2 us -> 0 us
    gather x456 -> x0, local copies, waits for them, and re-layouts: 198 us -> none
    ppermute x24 -> x0, starting transfers between devices: 63.8 us -> none  [the longest x12 48.3 us: with_halo(): before = lax.ppermute(last, axis, up)]
    all_gather x3 -> x0, blocking collectives: 33.9 us -> none  [the longest x1 19.9 us: local(): lax.all_gather(along_y, 'gz', axis=2, tiled=True).astype(jnp.float32)]
    reshape x3 -> x0, local copies, waits for them, and re-layouts: 27.3 us -> none  [the longest x1 26.6 us: coarsen(): weighted.reshape(comps, depth // 2, 2, width // 2, 2, height // 2, 2)]
    pallas_call x0 -> x1, Pallas kernels: none -> 25.4 us  [local(): pl.pallas_call(functools.partial(kernel, dims), out_shape=(jax.ShapeDtype...]
    ppermute x24 -> x0, waiting for transfers between devices: 24 us -> none  [the longest x12 15.3 us: with_halo(): after = lax.ppermute(leading, axis, down)]
    reduce_sum x5 -> x0, other arithmetic: 11.1 us -> none  [the longest x1 9.41 us: coarsen(): return jnp.mean(shaped, axis=(2, 4, 6)).astype(jnp.bfloat16)]
  transfers between devices with their start and end apart: 24 -> 0, of which waited for: 13 -> 0; matrix products, arithmetic and copies ran while one was open for 65% -> 0% of each run, Pallas kernels for 0% -> 0%
where the time goes in v1:
time: 30.5 us; the launch traced here: 30.2 us
  Pallas kernels  25.4 us (83%)
  local copies, waits for them, and re-layouts  4.1 us (13%)
  between operations  0.71 us (2%)
    pallas_call x1, Pallas kernels, local(): pl.pallas_call(functools.partial(kernel, dims), out_shape=(jax.ShapeDtype...  25.4 us
    unnamed x17, local copies, waits for them, and re-layouts  4.1 us

profile of v1, /device:TPU:0, one launch (start us, length us, event | category | flops | bytes accessed | tf_op | source)
XLA Modules:
  0.0 30.2 jit_solution(14810231467524755203)
XLA Ops:
  0.6 0.0 copy-start.4
  0.6 0.0 copy-start.2
  0.7 0.0 copy-start.3
  0.7 0.0 copy-start.6
  0.7 0.0 copy-start.5
  0.7 0.8 %copy.10.mix = f32[8,3,3]{2,1,0:T(4,128)S(1)} copy(f32[8,3,3]{0,2,1:T(4,128)} %param.15) | data formatting | bytes 576 | tf_op args[7]
  1.5 0.0 copy-done.4
  1.5 0.0 copy-done.2
  1.5 0.0 copy-done.3
  1.5 0.0 copy-done.6
  1.5 0.0 copy-done.5
  1.5 0.0 copy-start
  1.5 1.0 %copy-done = f32[3,4,32,256]{3,2,1,0:T(8,128)S(1)} copy-done((f32[3,4,32,256]{3,2,1,0:T(8,128)S(1)}, f32[3,4,32,256]{3,2,1,0:T(8,128)}, u32[]{:S(2)}) %copy-start) | copy-done | bytes 393240
  2.5 0.0 copy-start.1
  2.5 0.9 %copy-done.1 = s32[4,32,256]{2,1,0:T(8,128)S(1)} copy-done((s32[4,32,256]{2,1,0:T(8,128)S(1)}, s32[4,32,256]{2,1,0:T(8,128)}, u32[]{:S(2)}) %copy-start.1) | copy-done | bytes 131096
  3.4 25.4 %shard_map.95 = (f32[3,4,32,256]{3,2,1,0:T(8,128)S(1)}, f32[2,3,16,128]{3,2,1,0:T(8,128)S(1)}) custom-call(f32[3,4,32,256]{3,2,1,0:T(8,128)S(1)} %copy-done, s32[4,32,256]{2,1,0:T(8,128)S(1)} %copy-done.1, f32[16]{0:T(128)S(1)} %copy-done.5, f32[16]{0:T(128)S(1)} %copy-done.6, bf16[8,128]{1,0:T(8,128)(2,1)S(1)} %copy-done.3, bf16[8,512]{1,0:T(8,128)(2,1)S(1)} %copy-done.2, ...), custom_call_target="tpu_custom_call" | custom-call | tf_op jit(solution)/shard_map/pallas_call | solution.py:366
  28.9 0.7 %copy.13 = f32[3,4,32,256]{3,2,1,0:T(8,128)} copy(f32[3,4,32,256]{3,2,1,0:T(8,128)S(1)} %get-tuple-element.4) | data formatting | bytes 786432
  29.6 0.6 %copy.14 = f32[2,3,16,128]{3,2,1,0:T(8,128)} copy(f32[2,3,16,128]{3,2,1,0:T(8,128)S(1)} %get-tuple-element.5) | data formatting | bytes 98304
Async XLA Ops:
  0.6 0.9 %copy-start.4 = (bf16[8,16]{1,0:T(8,128)(2,1)S(1)}, bf16[8,16]{1,0:T(8,128)(2,1)}, u32[]{:S(2)}) copy-start(bf16[8,16]{1,0:T(8,128)(2,1)} %kz.1) | copy-start | bytes 772
  0.6 0.9 %copy-start.2 = (bf16[8,512]{1,0:T(8,128)(2,1)S(1)}, bf16[8,512]{1,0:T(8,128)(2,1)}, u32[]{:S(2)}) copy-start(bf16[8,512]{1,0:T(8,128)(2,1)} %ky.1) | copy-start | bytes 24580
  0.7 0.9 %copy-start.3 = (bf16[8,128]{1,0:T(8,128)(2,1)S(1)}, bf16[8,128]{1,0:T(8,128)(2,1)}, u32[]{:S(2)}) copy-start(bf16[8,128]{1,0:T(8,128)(2,1)} %kx.1) | copy-start | bytes 6148
  0.7 0.8 %copy-start.6 = (f32[16]{0:T(128)S(1)}, f32[16]{0:T(128)}, u32[]{:S(2)}) copy-start(f32[16]{0:T(128)} %sat_tab.1) | copy-start | bytes 196
  0.7 0.8 %copy-start.5 = (f32[16]{0:T(128)S(1)}, f32[16]{0:T(128)}, u32[]{:S(2)}) copy-start(f32[16]{0:T(128)} %stiff_tab.1) | copy-start | bytes 196
  1.5 1.0 %copy-start = (f32[3,4,32,256]{3,2,1,0:T(8,128)S(1)}, f32[3,4,32,256]{3,2,1,0:T(8,128)}, u32[]{:S(2)}) copy-start(f32[3,4,32,256]{3,2,1,0:T(8,128)} %magnet.1) | copy-start | bytes 1179652
  2.5 0.9 %copy-start.1 = (s32[4,32,256]{2,1,0:T(8,128)S(1)}, s32[4,32,256]{2,1,0:T(8,128)}, u32[]{:S(2)}) copy-start(s32[4,32,256]{2,1,0:T(8,128)} %grains.1) | copy-start | bytes 393220

commit v2 on v1

--- a/solution.py
+++ b/solution.py
@@ -19,15 +19,15 @@
 
 def kernel(
     dims,
-    magnet, grains, stiff_tab, sat_tab, kx, ky, kz, mix,
+    magnet_in, grains_in, stiff_tab, sat_tab, kx, ky, kz, mix,
     out_m, out_d,
-    state, stiff, inv_sat, weights, pooled_in, pooled, gathered, kx32, ky32, kz32, flat_x,
+    state, grains, stiff, inv_sat, weights, weight_x, weight_y, field_in, pooled_in, pooled, gathered, kx32, ky32, kz32, flat_x,
     mat_x, mat_y, trans_x, mixed, z_send, z_recv, fine,
     xs, xr, ys, yr, zs, zr,
-    g_send, g_recv, s_send, s_recv, h_send, h_recv,
+    g_send, g_recv, s_send, s_recv, h_send, h_recv, in_sem,
 ):
     cx, cy, cz = dims
-    comps, nz, nx, ny = magnet.shape
+    comps, nz, nx, ny = magnet_in.shape
     rank = kx.shape[0]
     mats = stiff_tab.shape[0]
     rz, rx, ry = nz // 2, nx // 2, ny // 2
@@ -40,6 +40,19 @@
     def spot(number):
         return lax.div(number, cy), lax.rem(number, cy)
 
+    def load(zc):
+        pair = pl.ds(2 * zc, 2)
+        return (
+            pltpu.make_async_copy(grains_in.at[pair], grains.at[pair], in_sem.at[zc, 0]),
+            pltpu.make_async_copy(
+                magnet_in.at[:, pair], state.at[0, :, pair], in_sem.at[zc, 1]
+            ),
+        )
+
+    for zc in range(rz):
+        for copy in load(zc):
+            copy.start()
+
     barrier = pltpu.get_barrier_semaphore()
     for d in range(1, plane):
         tx, ty = spot(lax.rem(me + d, plane))
@@ -56,22 +69,45 @@
     lane = lax.broadcasted_iota(jnp.int32, (nx, ny), 1)
     pack_lane = lax.broadcasted_iota(jnp.int32, (nx, LANES), 1)
 
+    kx32[...] = kx[...].astype(F32)
+    ky32[...] = ky[...].astype(F32)
+    kz32[...] = jnp.zeros_like(kz32)
+    kz32[:, 0:kz.shape[1]] = kz[...].astype(F32)
+
+    def skewed(line, width):
+        rows = jnp.broadcast_to(line, (8, width))
+        place = lax.broadcasted_iota(jnp.int32, (8, width), 0)
+        for step in (1, 2, 4):
+            rows = jnp.where(place & step != 0, pltpu.roll(rows, step, 1), rows)
+        return rows
+
+    wide = 2 * gx_all
+    lane_x = lax.broadcasted_iota(jnp.int32, (8, wide), 1)
+    kx_here = pltpu.roll(kx32[...], lax.rem(2 * wide - gx_all - ix * rx, wide), 1)
+    bases = [skewed(kx_here[r:r + 1, :], wide) for r in range(rank)]
+    for t in range(gx_all // 8):
+        block = jnp.zeros((8, wide), F32)
+        for r in range(rank):
+            turned = pltpu.roll(bases[r], (8 * t + r * rx) % wide, 1)
+            block = jnp.where(lane_x // rx == r, turned, block)
+        flat_x[8 * t:8 * t + 8, :] = block[:, 0:rank * rx]
+    mat_x[...] = jnp.transpose(flat_x[...]).astype(BF16)
+    def lookup(g, table):
+        value = jnp.full((nx, ny), table[0], F32)
+        for k in range(1, mats):
+            value = jnp.where(g == k, table[k], value)
+        return value
+
     for zc in range(rz):
+        for copy in load(zc):
+            copy.wait()
         sums = [None] * comps
         for half in range(2):
             z = 2 * zc + half
-            g = grains[z]
-            a = jnp.full((nx, ny), stiff_tab[0], F32)
-            s = jnp.full((nx, ny), sat_tab[0], F32)
-            for k in range(1, mats):
-                hit = g == k
-                a = jnp.where(hit, stiff_tab[k], a)
-                s = jnp.where(hit, sat_tab[k], s)
-            stiff[z] = a
+            s = lookup(grains[z], sat_tab)
             inv_sat[z] = 2.0 / s
             for j in range(comps):
-                m = magnet[j, z]
-                state[0, j, z + 1] = m
+                m = state[0, j, z]
                 sums[j] = s * m if half == 0 else sums[j] + s * m
         for j in range(comps):
             pooled_in[(j * rz + zc) * nx:(j * rz + zc + 1) * nx, :] = sums[j]
@@ -93,6 +129,20 @@
 
     block_of(ix, iy)[...] = coarse.astype(BF16).reshape(jz, rx, ry)
 
+    pl.semaphore_wait(barrier, plane - 1 + cz - 1)
+
+    def gather_copy(d, source):
+        px, py = spot(source)
+        tx, ty = spot(lax.rem(me + d, plane))
+        return pltpu.make_async_remote_copy(
+            src_ref=block_of(px, py), dst_ref=block_of(px, py),
+            send_sem=g_send.at[d - 1], recv_sem=g_recv.at[d - 1],
+            device_id={"gx": tx, "gy": ty, "gz": iz}, device_id_type=MESH,
+        )
+
+    for d in range(1, plane):
+        gather_copy(d, me).start()
+
     def pack(step, k, value, edges):
         xs[step, 0, k:k + 1, :] = value[0:1, :]
         xs[step, 1, k:k + 1, :] = value[nx - 1:nx, :]
@@ -102,30 +152,18 @@
             jnp.where(hit, value[:, ny - 1:ny], edges[1]),
         )
 
+    for z in range(nz):
+        stiff[z] = lookup(grains[z], stiff_tab)
     edges = (jnp.zeros((nx, LANES), F32),) * 2
     for j in range(comps + 1):
         for z in range(nz):
-            value = magnet[j, z] if j < comps else stiff[z]
+            value = state[0, j, z] if j < comps else stiff[z]
             edges = pack(0, j * nz + z, value, edges)
             if z == 0:
                 zs[0, 0, j] = value.astype(BF16)
             if z == nz - 1:
                 zs[0, 1, j] = value.astype(BF16)
     ys[0, 0], ys[0, 1] = edges
-
-    pl.semaphore_wait(barrier, plane - 1 + cz - 1)
-
-    def gather_copy(d, source):
-        px, py = spot(source)
-        tx, ty = spot(lax.rem(me + d, plane))
-        return pltpu.make_async_remote_copy(
-            src_ref=block_of(px, py), dst_ref=block_of(px, py),
-            send_sem=g_send.at[d - 1], recv_sem=g_recv.at[d - 1],
-            device_id={"gx": tx, "gy": ty, "gz": iz}, device_id_type=MESH,
-        )
-
-    for d in range(1, plane):
-        gather_copy(d, me).start()
 
     places = (ix, iy, iz)
     counts = (cx, cy, cz)
@@ -147,8 +185,8 @@
     def can_send(axis, way):
         return places[axis] > 0 if way == 0 else places[axis] < counts[axis] - 1
 
-    def send_halos(step):
-        for axis in (2, 1, 0):
+    def send_halos(step, axes):
+        for axis in axes:
             for way in range(2):
                 @pl.when(can_send(axis, way))
                 def _():
@@ -161,7 +199,7 @@
                 def _():
                     halo_copy(step, axis, way).wait_recv()
 
-    send_halos(0)
+    send_halos(0, (2, 1, 0))
 
     for axis in range(3):
         recvs = (xr, yr, zr)[axis]
@@ -171,29 +209,6 @@
                 for step in range(SUBSTEPS):
                     recvs[step, way] = jnp.zeros(recvs.shape[2:], recvs.dtype)
 
-    kx32[...] = kx[...].astype(F32)
-    ky32[...] = ky[...].astype(F32)
-    kz32[...] = jnp.zeros_like(kz32)
-    kz32[:, 0:kz.shape[1]] = kz[...].astype(F32)
-
-    def skewed(line, width):
-        rows = jnp.broadcast_to(line, (8, width))
-        place = lax.broadcasted_iota(jnp.int32, (8, width), 0)
-        for step in (1, 2, 4):
-            rows = jnp.where(place & step != 0, pltpu.roll(rows, step, 1), rows)
-        return rows
-
-    wide = 2 * gx_all
-    lane_x = lax.broadcasted_iota(jnp.int32, (8, wide), 1)
-    kx_here = pltpu.roll(kx32[...], lax.rem(2 * wide - gx_all - ix * rx, wide), 1)
-    bases = [skewed(kx_here[r:r + 1, :], wide) for r in range(rank)]
-    for t in range(gx_all // 8):
-        block = jnp.zeros((8, wide), F32)
-        for r in range(rank):
-            turned = pltpu.roll(bases[r], (8 * t + r * rx) % wide, 1)
-            block = jnp.where(lane_x // rx == r, turned, block)
-        flat_x[8 * t:8 * t + 8, :] = block[:, 0:rank * rx]
-    mat_x[...] = jnp.transpose(flat_x[...]).astype(BF16)
     for c in range(cy):
         start = pl.multiple_of(ry * (iy - c) + gy_all - ry, ry)
         window = ky32[:, pl.ds(start, 2 * ry)]
@@ -215,62 +230,103 @@
         along = jnp.dot(trans_x[r], mat_y[r], preferred_element_type=F32)
         along = along.astype(BF16).astype(F32).reshape(comps, rz, rx, ry)
         for i in range(comps):
-            total = mix[r, i, 0] * along[0]
+            total = mix[i, 0, r] * along[0]
             for j in range(1, comps):
-                total = total + mix[r, i, j] * along[j]
+                total = total + mix[i, j, r] * along[j]
             mixed[r, i] = total
-    turned_z = pltpu.roll(kz32[...], lax.rem(LANES + rz - 1 + rz * iz - gz_all, LANES), 1)
-
     def sum_copy(peer, slot):
         return pltpu.make_async_remote_copy(
             src_ref=z_send.at[peer], dst_ref=z_recv.at[slot],
             send_sem=s_send.at[peer], recv_sem=s_recv.at[slot],
-            device_id={"gx": ix, "gy": iy, "gz": jnp.int32(peer)}, device_id_type=MESH,
-        )
-
-    for p in range(cz):
+            device_id={"gx": ix, "gy": iy, "gz": peer}, device_id_type=MESH,
+        )
+
+    for n in range(cz):
+        d = (cz // 2 + n) % cz if n < cz - cz // 2 else cz - n - 1
+        p = lax.rem(iz + d, cz) if d else iz
+        turn = lax.rem(2 * LANES + rz - 1 + rz * (iz - p) - gz_all, LANES)
+        turned_z = pltpu.roll(kz32[...], turn, 1)
         totals = [[jnp.zeros((rx, ry), F32) for _ in range(comps)] for _ in range(rz)]
         for r in range(rank):
             for al in range(rz):
                 for zl in range(rz):
-                    at = p * rz + al - zl + rz - 1
+                    at = al - zl + rz - 1
                     factor = turned_z[r:r + 1, at:at + 1]
                     for i in range(comps):
                         totals[al][i] = totals[al][i] + factor * mixed[r, i, zl]
+        target = z_send if d else z_recv
         for al in range(rz):
             for i in range(comps):
-                z_send[p, al, i] = totals[al][i]
-
-        @pl.when(iz != p)
-        def _():
+                target[p, al, i] = totals[al][i]
+        if d:
             sum_copy(p, iz).start()
 
-        @pl.when(iz == p)
-        def _():
-            z_recv[p] = z_send[p]
-
     receive_halos(0)
 
-    def around(value, step, k):
+    def rolled(value):
         return (
-            jnp.where(row == 0, xr[step, 0, k:k + 1, :], pltpu.roll(value, 1, 0)),
-            jnp.where(row == nx - 1, xr[step, 1, k:k + 1, :], pltpu.roll(value, nx - 1, 0)),
-            jnp.where(lane == 0, yr[step, 0][:, k:k + 1], pltpu.roll(value, 1, 1)),
-            jnp.where(lane == ny - 1, yr[step, 1][:, k:k + 1], pltpu.roll(value, ny - 1, 1)),
-        )
-
+            pltpu.roll(value, 1, 0), pltpu.roll(value, nx - 1, 0),
+            pltpu.roll(value, 1, 1), pltpu.roll(value, ny - 1, 1),
+        )
+
+    row_top = lax.broadcasted_iota(jnp.int32, (8, ny), 0)
     for z in range(nz):
         here = stiff[z]
+        k = comps * nz + z
         below = zr[0, 0, comps].astype(F32) if z == 0 else stiff[z - 1]
         above = zr[0, 1, comps].astype(F32) if z == nz - 1 else stiff[z + 1]
         scale = 2.0 * inv_sat[z] * here
-        for n, near in enumerate(around(here, 0, comps * nz + z) + (below, above)):
-            weights[n, z] = scale * near / (here + near)
+        outside = (row == 0, row == nx - 1, lane == 0, lane == ny - 1)
+        for n, near in enumerate(rolled(here)):
+            weights[n, z] = jnp.where(outside[n], 0.0, scale * near / (here + near))
+        weights[4, z] = scale * below / (here + below)
+        weights[5, z] = scale * above / (here + above)
+        for way in range(2):
+            cut = slice(0, 8) if way == 0 else slice(nx - 8, nx)
+            near = xr[0, way, k:k + 1, :]
+            weight_x[way, z] = jnp.where(
+                row_top == 7 * way, scale[cut] * near / (here[cut] + near), 0.0
+            )
+            cut = slice(0, LANES) if way == 0 else slice(ny - LANES, ny)
+            near = yr[0, way][:, k:k + 1]
+            weight_y[way, z] = jnp.where(
+                pack_lane == (LANES - 1) * way,
+                scale[:, cut] * near / (here[:, cut] + near), 0.0,
+            )
+
+    def inner_field(now, z, j):
+        near = rolled(state[now, j, z])
+        field = weights[0, z] * near[0]
+        for n in range(1, 4):
+            field = field + weights[n, z] * near[n]
+        if z > 0:
+            field = field + weights[4, z] * state[now, j, z - 1]
+        if z < nz - 1:
+            field = field + weights[5, z] * state[now, j, z + 1]
+        return field
+
+    def outer_field(field, step, z, j):
+        k = j * nz + z
+        if z == 0:
+            field = field + weights[4, z] * zr[step, 0, j].astype(F32)
+        if z == nz - 1:
+            field = field + weights[5, z] * zr[step, 1, j].astype(F32)
+        top = field[0:8] + weight_x[0, z] * xr[step, 0, k:k + 1, :]
+        bottom = field[nx - 8:nx] + weight_x[1, z] * xr[step, 1, k:k + 1, :]
+        field = jnp.concatenate([top, field[8:nx - 8], bottom], axis=0)
+        left = field[:, 0:LANES] + weight_y[0, z] * yr[step, 0][:, k:k + 1]
+        right = field[:, ny - LANES:ny] + weight_y[1, z] * yr[step, 1][:, k:k + 1]
+        middle = [field[:, LANES:ny - LANES]] if ny > 2 * LANES else []
+        return jnp.concatenate([left] + middle + [right], axis=1)
+
+    for z in range(nz):
+        for j in range(comps):
+            field_in[j, z] = outer_field(inner_field(0, z, j), 0, z, j)
 
     for p in range(cz):
         @pl.when(iz != p)
         def _():
-            sum_copy(p, p).wait_recv()
+            sum_copy(jnp.int32(p), p).wait_recv()
 
     total = z_recv[0]
     for p in range(1, cz):
@@ -289,28 +345,25 @@
         for odd in range(2):
             fine.at[part][pl.ds(odd, rz * comps * rx, 2), :] = piece
 
+    def demag_at(z, j):
+        at = ((z // 2) * comps + j) * nx
+        return jnp.concatenate([fine[0, at:at + nx, :], fine[1, at:at + nx, :]], axis=1)
+
     for step in range(SUBSTEPS):
         now, later = step % 2, (step + 1) % 2
         last = step == SUBSTEPS - 1
         if step > 0:
             receive_halos(step)
-        for j in range(comps):
-            state[now, j, 0] = zr[step, 0, j].astype(F32)
-            state[now, j, nz + 1] = zr[step, 1, j].astype(F32)
         edges = (jnp.zeros((nx, LANES), F32),) * 2
-        for z in range(nz):
+        for z in [0, nz - 1] + list(range(1, nz - 1)):
             m, h = [], []
             for j in range(comps):
-                value = state[now, j, z + 1]
-                at = ((z // 2) * comps + j) * nx
-                field = jnp.concatenate([fine[0, at:at + nx, :], fine[1, at:at + nx, :]], axis=1)
-                near = around(value, step, j * nz + z) + (
-                    state[now, j, z], state[now, j, z + 2]
-                )
-                for n in range(6):
-                    field = field + weights[n, z] * near[n]
-                m.append(value)
-                h.append(field)
+                m.append(state[now, j, z])
+                field = field_in[j, z]
+                if step == 0:
+                    h.append(field + demag_at(z, j))
+                else:
+                    h.append(outer_field(field, step, z, j))
             t = [
                 m[1] * h[2] - m[2] * h[1],
                 m[2] * h[0] - m[0] * h[2],
@@ -328,22 +381,27 @@
                 if last:
                     out_m[j, z] = value
                     continue
-                state[later, j, z + 1] = value
+                state[later, j, z] = value
                 edges = pack(step + 1, j * nz + z, value, edges)
                 if z == 0:
                     zs[step + 1, 0, j] = value.astype(BF16)
                 if z == nz - 1:
                     zs[step + 1, 1, j] = value.astype(BF16)
+            if z == nz - 1 and not last:
+                send_halos(step + 1, (2,))
         if not last:
             ys[step + 1, 0], ys[step + 1, 1] = edges
-            send_halos(step + 1)
+            send_halos(step + 1, (1, 0))
+            for z in range(nz):
+                for j in range(comps):
+                    field_in[j, z] = inner_field(later, z, j) + demag_at(z, j)
 
     for d in range(1, plane):
         gather_copy(d, me).wait_send()
     for p in range(cz):
         @pl.when(iz != p)
         def _():
-            sum_copy(p, iz).wait_send()
+            sum_copy(jnp.int32(p), iz).wait_send()
     for step in range(SUBSTEPS):
         for axis in range(3):
             for way in range(2):
@@ -361,6 +419,7 @@
     gx_all, gy_all = rx * cx, ry * cy
     packed = (comps + 1) * nz
     vmem = pl.BlockSpec(memory_space=pltpu.VMEM)
+    hbm = pl.BlockSpec(memory_space=pltpu.HBM)
     smem = pl.BlockSpec(memory_space=pltpu.SMEM)
     dma = pltpu.SemaphoreType.DMA
     return pl.pallas_call(
@@ -369,13 +428,17 @@
             jax.ShapeDtypeStruct(magnet.shape, F32),
             jax.ShapeDtypeStruct((rz, comps, rx, ry), F32),
         ),
-        in_specs=[vmem, vmem, smem, smem, vmem, vmem, vmem, smem],
+        in_specs=[hbm, hbm, smem, smem, vmem, vmem, vmem, smem],
         out_specs=(vmem, vmem),
         scratch_shapes=[
-            pltpu.VMEM((2, comps, nz + 2, nx, ny), F32),
+            pltpu.VMEM((2, comps, nz, nx, ny), F32),
+            pltpu.VMEM((nz, nx, ny), jnp.int32),
             pltpu.VMEM((nz, nx, ny), F32),
             pltpu.VMEM((nz, nx, ny), F32),
             pltpu.VMEM((6, nz, nx, ny), F32),
+            pltpu.VMEM((2, nz, 8, ny), F32),
+            pltpu.VMEM((2, nz, nx, LANES), F32),
+            pltpu.VMEM((comps, nz, nx, ny), F32),
             pltpu.VMEM((jz * nx, ny), F32),
             pltpu.VMEM((jz * nx, ry), F32),
             pltpu.VMEM((jz, gx_all, gy_all), BF16),
@@ -402,11 +465,12 @@
             dma((cz,)),
             dma((SUBSTEPS, 3, 2)),
             dma((SUBSTEPS, 3, 2)),
+            dma((rz, 2)),
         ],
         compiler_params=pltpu.CompilerParams(
-            collective_id=0, has_side_effects=True, vmem_limit_bytes=40 * 1024 * 1024
+            collective_id=0, has_side_effects=True, vmem_limit_bytes=56 * 1024 * 1024
         ),
-    )(magnet, grains, stiff_tab, sat_tab, kx, ky, kz, mix)
+    )(magnet, grains, stiff_tab, sat_tab, kx, ky, kz, jnp.transpose(mix, (1, 2, 0)))
 
 
 def solution(mesh):

time: 30.5 us -> 28.6 us (0.938)
  local copies, waits for them, and re-layouts: 4.1 us -> 2.4 us
    unnamed x17 -> x4, local copies, waits for them, and re-layouts: 4.1 us -> 2.4 us
where the time goes in v2:
time: 28.6 us; the launch traced here: 28.4 us
  Pallas kernels  25.4 us (89%)
  local copies, waits for them, and re-layouts  2.4 us (8%)
  between operations  0.65 us (2%)
    pallas_call x1, Pallas kernels, local(): pl.pallas_call(functools.partial(kernel, dims), out_shape=(jax.ShapeDtype...  25.4 us
    unnamed x4, local copies, waits for them, and re-layouts  2.4 us

profile of v2, /device:TPU:0, one launch (start us, length us, event | category | flops | bytes accessed | tf_op | source)
XLA Modules:
  0.0 28.4 jit_solution(3627901416023937497)
XLA Ops:
  0.6 25.4 %shard_map.95 = (f32[3,4,32,256]{3,2,1,0:T(8,128)}, f32[2,3,16,128]{3,2,1,0:T(8,128)}) custom-call(f32[3,4,32,256]{3,2,1,0:T(8,128)} %magnet_in.1, s32[4,32,256]{2,1,0:T(8,128)} %grains_in.1, f32[16]{0:T(128)} %stiff_tab.1, f32[16]{0:T(128)} %sat_tab.1, bf16[8,128]{1,0:T(8,128)(2,1)} %kx.1, bf16[8,512]{1,0:T(8,128)(2,1)} %ky.1, bf16[8,16]{1,0:T(8,128)(2,1)} %kz.1, ...), custom_call_target="tpu_custom_call" | custom-call | tf_op jit(solution)/shard_map/pallas_call | solution.py:425
  26.0 0.0 copy-start
  26.0 1.8 %copy.12 = f32[3,4,32,256]{3,2,1,0:T(8,128)} copy(f32[3,4,32,256]{3,2,1,0:T(8,128)} %get-tuple-element.4) | data formatting | bytes 786432
  27.8 0.0 copy-done
  27.8 0.6 %copy.13 = f32[2,3,16,128]{3,2,1,0:T(8,128)} copy(f32[2,3,16,128]{3,2,1,0:T(8,128)S(1)} %copy-done) | data formatting | bytes 98304
Async XLA Ops:
  26.0 1.8 %copy-start = (f32[2,3,16,128]{3,2,1,0:T(8,128)S(1)}, f32[2,3,16,128]{3,2,1,0:T(8,128)}, u32[]{:S(2)}) copy-start(f32[2,3,16,128]{3,2,1,0:T(8,128)} %get-tuple-element.5) | copy-start | bytes 147460

commit v3 on v2

--- a/solution.py
+++ b/solution.py
@@ -425,8 +425,8 @@
     return pl.pallas_call(
         functools.partial(kernel, dims),
         out_shape=(
-            jax.ShapeDtypeStruct(magnet.shape, F32),
-            jax.ShapeDtypeStruct((rz, comps, rx, ry), F32),
+            pltpu.VMEM(magnet.shape, F32),
+            pltpu.VMEM((rz, comps, rx, ry), F32),
         ),
         in_specs=[hbm, hbm, smem, smem, vmem, vmem, vmem, smem],
         out_specs=(vmem, vmem),

time: 28.6 us -> 26.8 us (0.937)
  local copies, waits for them, and re-layouts: 2.4 us -> 1.37 us
  Pallas kernels: 25.4 us -> 24.6 us
    unnamed x4 -> x2, local copies, waits for them, and re-layouts: 2.4 us -> 1.37 us
    pallas_call x1, Pallas kernels: 25.4 us -> 24.6 us  [local(): pl.pallas_call(functools.partial(kernel, dims), out_shape=(pltpu.VMEM(mag...]
where the time goes in v3:
time: 26.8 us; the launch traced here: 26.6 us
  Pallas kernels  24.6 us (92%)
  local copies, waits for them, and re-layouts  1.37 us (5%)
  between operations  0.64 us (2%)
    pallas_call x1, Pallas kernels, local(): pl.pallas_call(functools.partial(kernel, dims), out_shape=(pltpu.VMEM(mag...  24.6 us
    unnamed x2, local copies, waits for them, and re-layouts  1.37 us

profile of v3, /device:TPU:0, one launch (start us, length us, event | category | flops | bytes accessed | tf_op | source)
XLA Modules:
  0.0 26.6 jit_solution(10775025886083279335)
XLA Ops:
  0.6 24.6 %shard_map.95 = (f32[3,4,32,256]{3,2,1,0:T(8,128)S(1)}, f32[2,3,16,128]{3,2,1,0:T(8,128)S(1)}) custom-call(f32[3,4,32,256]{3,2,1,0:T(8,128)} %magnet_in.1, s32[4,32,256]{2,1,0:T(8,128)} %grains_in.1, f32[16]{0:T(128)} %stiff_tab.1, f32[16]{0:T(128)} %sat_tab.1, bf16[8,128]{1,0:T(8,128)(2,1)} %kx.1, bf16[8,512]{1,0:T(8,128)(2,1)} %ky.1, bf16[8,16]{1,0:T(8,128)(2,1)} %kz.1, ...), custom_call_target="tpu_custom_call" | custom-call | tf_op jit(solution)/shard_map/pallas_call | solution.py:425
  25.3 0.7 %copy.12 = f32[3,4,32,256]{3,2,1,0:T(8,128)} copy(f32[3,4,32,256]{3,2,1,0:T(8,128)S(1)} %get-tuple-element.2) | data formatting | bytes 786432
  26.0 0.6 %copy.13 = f32[2,3,16,128]{3,2,1,0:T(8,128)} copy(f32[2,3,16,128]{3,2,1,0:T(8,128)S(1)} %get-tuple-element.3) | data formatting | bytes 98304

commit v4 on v3

--- a/solution.py
+++ b/solution.py
@@ -17,10 +17,41 @@
 BF16 = jnp.bfloat16
 
 
+def precess(m, h):
+    comps = len(m)
+    t = [
+        m[1] * h[2] - m[2] * h[1],
+        m[2] * h[0] - m[0] * h[2],
+        m[0] * h[1] - m[1] * h[0],
+    ]
+    u = [
+        m[1] * t[2] - m[2] * t[1],
+        m[2] * t[0] - m[0] * t[2],
+        m[0] * t[1] - m[1] * t[0],
+    ]
+    raw = [m[j] - TIME_STEP * (t[j] + DAMPING * u[j]) for j in range(comps)]
+    shrink = lax.rsqrt(raw[0] * raw[0] + raw[1] * raw[1] + raw[2] * raw[2])
+    return [part * shrink for part in raw]
+
+
+def finish(m, h, demag, out_m, out_d, held, sems):
+    comps, nz = m.shape[:2]
+    copies = [pltpu.make_async_copy(demag, out_d, sems.at[nz])]
+    copies[0].start()
+    for z in range(nz):
+        new = precess([m[j, z] for j in range(comps)], [h[j, z] for j in range(comps)])
+        for j in range(comps):
+            held[j, z] = new[j]
+        copies.append(pltpu.make_async_copy(held.at[:, z], out_m.at[:, z], sems.at[z]))
+        copies[-1].start()
+    for copy in copies:
+        copy.wait()
+
+
 def kernel(
     dims,
     magnet_in, grains_in, stiff_tab, sat_tab, kx, ky, kz, mix,
-    out_m, out_d,
+    out_m, out_h, out_d,
     state, grains, stiff, inv_sat, weights, weight_x, weight_y, field_in, pooled_in, pooled, gathered, kx32, ky32, kz32, flat_x,
     mat_x, mat_y, trans_x, mixed, z_send, z_recv, fine,
     xs, xr, ys, yr, zs, zr,
@@ -185,9 +216,9 @@
     def can_send(axis, way):
         return places[axis] > 0 if way == 0 else places[axis] < counts[axis] - 1
 
-    def send_halos(step, axes):
+    def send_halos(step, axes, ways=(0, 1)):
         for axis in axes:
-            for way in range(2):
+            for way in ways:
                 @pl.when(can_send(axis, way))
                 def _():
                     halo_copy(step, axis, way).start()
@@ -364,31 +395,23 @@
                     h.append(field + demag_at(z, j))
                 else:
                     h.append(outer_field(field, step, z, j))
-            t = [
-                m[1] * h[2] - m[2] * h[1],
-                m[2] * h[0] - m[0] * h[2],
-                m[0] * h[1] - m[1] * h[0],
-            ]
-            u = [
-                m[1] * t[2] - m[2] * t[1],
-                m[2] * t[0] - m[0] * t[2],
-                m[0] * t[1] - m[1] * t[0],
-            ]
-            raw = [m[j] - TIME_STEP * (t[j] + DAMPING * u[j]) for j in range(comps)]
-            shrink = lax.rsqrt(raw[0] * raw[0] + raw[1] * raw[1] + raw[2] * raw[2])
+            if last:
+                for j in range(comps):
+                    out_m[j, z], out_h[j, z] = m[j], h[j]
+                continue
+            turned_m = precess(m, h)
             for j in range(comps):
-                value = raw[j] * shrink
-                if last:
-                    out_m[j, z] = value
-                    continue
+                value = turned_m[j]
                 state[later, j, z] = value
                 edges = pack(step + 1, j * nz + z, value, edges)
                 if z == 0:
                     zs[step + 1, 0, j] = value.astype(BF16)
                 if z == nz - 1:
                     zs[step + 1, 1, j] = value.astype(BF16)
-            if z == nz - 1 and not last:
-                send_halos(step + 1, (2,))
+            if not last and z == 0:
+                send_halos(step + 1, (2,), (0,))
+            if not last and z == nz - 1:
+                send_halos(step + 1, (2,), (1,))
         if not last:
             ys[step + 1, 0], ys[step + 1, 1] = edges
             send_halos(step + 1, (1, 0))
@@ -422,14 +445,15 @@
     hbm = pl.BlockSpec(memory_space=pltpu.HBM)
     smem = pl.BlockSpec(memory_space=pltpu.SMEM)
     dma = pltpu.SemaphoreType.DMA
-    return pl.pallas_call(
+    m, h, demag = pl.pallas_call(
         functools.partial(kernel, dims),
         out_shape=(
+            pltpu.VMEM(magnet.shape, F32),
             pltpu.VMEM(magnet.shape, F32),
             pltpu.VMEM((rz, comps, rx, ry), F32),
         ),
         in_specs=[hbm, hbm, smem, smem, vmem, vmem, vmem, smem],
-        out_specs=(vmem, vmem),
+        out_specs=(vmem, vmem, vmem),
         scratch_shapes=[
             pltpu.VMEM((2, comps, nz, nx, ny), F32),
             pltpu.VMEM((nz, nx, ny), jnp.int32),
@@ -471,6 +495,16 @@
             collective_id=0, has_side_effects=True, vmem_limit_bytes=56 * 1024 * 1024
         ),
     )(magnet, grains, stiff_tab, sat_tab, kx, ky, kz, jnp.transpose(mix, (1, 2, 0)))
+    return pl.pallas_call(
+        finish,
+        out_shape=(
+            jax.ShapeDtypeStruct(m.shape, F32), jax.ShapeDtypeStruct(demag.shape, F32)
+        ),
+        in_specs=[vmem, vmem, vmem],
+        out_specs=(hbm, hbm),
+        scratch_shapes=[pltpu.VMEM(m.shape, F32), dma((nz + 1,))],
+        compiler_params=pltpu.CompilerParams(vmem_limit_bytes=8 * 1024 * 1024),
+    )(m, h, demag)
 
 
 def solution(mesh):

time: 26.8 us -> 26.2 us (0.978)
  local copies, waits for them, and re-layouts: 1.37 us -> 0 us
  Pallas kernels: 24.6 us -> 25.3 us
    unnamed x2 -> x0, local copies, waits for them, and re-layouts: 1.37 us -> none
    pallas_call x0 -> x1, Pallas kernels: none -> 0.86 us  [local(): pl.pallas_call(finish, out_shape=(jax.ShapeDtypeStruct(m.shape, F32), jax...]
where the time goes in v4:
time: 26.2 us; the launch traced here: 26 us
  Pallas kernels  25.3 us (97%)
  between operations  0.64 us (2%)
    pallas_call x1, Pallas kernels, local(): pl.pallas_call(functools.partial(kernel, dims), out_shape=(pltpu.VMEM(mag...  24.5 us
    pallas_call x1, Pallas kernels, local(): pl.pallas_call(finish, out_shape=(jax.ShapeDtypeStruct(m.shape, F32), jax...  0.86 us

profile of v4, /device:TPU:0, one launch (start us, length us, event | category | flops | bytes accessed | tf_op | source)
XLA Modules:
  0.0 26.0 jit_solution(18423747885678396677)
XLA Ops:
  0.6 24.5 %shard_map.95 = (f32[3,4,32,256]{3,2,1,0:T(8,128)S(1)}, f32[3,4,32,256]{3,2,1,0:T(8,128)S(1)}, f32[2,3,16,128]{3,2,1,0:T(8,128)S(1)}) custom-call(f32[3,4,32,256]{3,2,1,0:T(8,128)} %magnet_in.1, s32[4,32,256]{2,1,0:T(8,128)} %grains_in.1, f32[16]{0:T(128)} %stiff_tab.1, f32[16]{0:T(128)} %sat_tab.1, bf16[8,128]{1,0:T(8,128)(2,1)} %kx.1, bf16[8,512]{1,0:T(8,128)(2,1)} %ky.1, ...), custom_call_target="tpu_custom_call" | custom-call | tf_op jit(solution)/shard_map/pallas_call | solution.py:448
  25.1 0.9 %shard_map.96 = (f32[3,4,32,256]{3,2,1,0:T(8,128)}, f32[2,3,16,128]{3,2,1,0:T(8,128)}) custom-call(f32[3,4,32,256]{3,2,1,0:T(8,128)S(1)} %get-tuple-element.5.m, f32[3,4,32,256]{3,2,1,0:T(8,128)S(1)} %get-tuple-element.6.h, f32[2,3,16,128]{3,2,1,0:T(8,128)S(1)} %get-tuple-element.7.demag), custom_call_target="tpu_custom_call" | custom-call | tf_op jit(solution)/shard_map/pallas_call | solution.py:498
